TPU v7x, 128 devices: a whole 4x4x4 slice. The times are simulated.
128 devices in a mesh: group: 8 (over y, core), tp: 16 (over x, z).
Axes of the slice: x: 4, y: 4, z: 4, core: 2. Of those that a mesh axis runs over, the one named last changes fastest.
Arguments:
- residual: bfloat16 [768, 4096], P('group', 'tp'), may hold values from -18 to 18
- tree_qkv: bfloat16 [3, 768, 4096], P(None, 'group', 'tp'), may hold values from -12.5 to 12.5
- kv_pool: bfloat16 [2, 256, 128, 4096], P(None, 'group', None, 'tp'), may hold values from -12.5 to 12.5
- page_table: int32 [16, 28], replicated, may hold values from 0 to 31, as said below
- cache_len: int32 [16], replicated, may hold values from 1 to 3584, as said below
- tree_parent: int32 [16, 48], replicated, may hold values from 0 to 46, as said below
- accepted_nodes: int32 [16, 4], P('group'), may hold values from 0 to 47
- out_weight: bfloat16 [4096, 4096], P('tp'), may hold values from -0.125 to 0.125
- norm_gain: float32 [4096], P('tp'), may hold values from 0.5 to 1.5
- draft_weight: bfloat16 [3, 4096, 4096], P(None, None, 'tp'), may hold values from -0.09375 to 0.09375
- vocab_weight: bfloat16 [26624, 4096], P('tp'), may hold values from -1.75 to 1.75
- target_ids: int32 [4, 768], P(None, 'group'), may hold values from 0 to 26623
Outputs:
- log_probs: float32 [4, 768], P(None, 'group')
- accepted_kv: bfloat16 [2, 64, 4096], P(None, 'group', 'tp')
Inputs may be any that keep to these rules, and one draw needn't show every extreme that they name: `cache_len`: request 2 g is group g's short request and request 2 g + 1 its long one; a short request has at most 512 positions and some group's has exactly that many; a long request has 128 or more and some group's has exactly 3584. `page_table`: entries of request r of group g = r // 2 are slots of group g's pool, except the odd columns of a long request, which are slots of group g xor 1's pool. In each group's pool the short request's first 4 columns, its long request's even columns and the odd columns of group g xor 1's long request are distinct slots covering the pool; a short request's columns from 4 on repeat its first ones. `tree_parent`: node 0 is the root and its own parent; every other node's parent has a smaller index, and node 48 - 1's parent is node 46.
All inputs are finite; a program needn't handle non-finite values.
Results may differ from a plain program's by a relative error of at most 0.004.
Values may be sent and summed in bfloat16 or wider, within the bound.
A program may use at most 128 MiB of HBM per device.

v0:
```python
import math
import jax
import jax.numpy as jnp
from jax import lax
from jax.sharding import PartitionSpec as P

D = 4096
HEADS = 32
HD = 128
TREE = 48
SHORT_PAGES = 4
LONG_PAGES = 28
EPSILON = 1e-05


def from_partner(block, axis, apart):
    count = lax.axis_size(axis)
    route = []
    for low in range(count):
        high = low | 1 << apart
        if high != low and high < count:
            route += [(low, high), (high, low)]
    return lax.ppermute(block, axis, route)


def combined_all(array, axis, combine):
    everything = jax.tree.map(lambda part: lax.all_gather(part, axis), array)
    leading = jax.tree.map(lambda part: part[0], everything)

    def turn(k, so_far):
        return combine(so_far, jax.tree.map(lambda part: part[k], everything))

    return lax.fori_loop(1, lax.axis_size(axis), turn, leading)


def ancestry(parents):
    number = parents.shape[0]
    indices = jnp.arange(number, dtype=jnp.int32)
    linked = ((parents[:, None] == indices[None, :]) & (indices[:, None] > 0)).astype(jnp.float32)
    reached = jnp.minimum(jnp.eye(number, dtype=jnp.float32) + linked, 1.0)
    for sweep_index in range(max(1, number.bit_length())):
        reached = jnp.minimum(jnp.dot(reached, reached, precision=lax.Precision.HIGHEST), 1.0)
    depths = jnp.sum(reached, axis=1) - 1.0
    return (reached, depths)


def slope_values(first, number):
    ordinal = jnp.arange(number, dtype=jnp.float32) + jnp.asarray(first, jnp.float32) + 1.0
    return jnp.exp2(-8.0 * ordinal / HEADS)


def partial_attention(queries, key_rows, value_rows, allowed, query_pos, key_pos, slopes):
    scores = jnp.einsum("thd,lhd->htl", queries, key_rows, preferred_element_type=jnp.float32) * (
        1.0 / math.sqrt(HD)
    )
    scores = scores - slopes[:, None, None] * (query_pos[None, :, None] - key_pos[None, None, :])
    row_top = jnp.max(jnp.where(allowed[None], scores, -1e30), axis=2)
    weights = jnp.where(allowed[None], jnp.exp(scores - row_top[:, :, None]), 0.0)
    weight_sum = jnp.sum(weights, axis=2)
    weighted = jnp.einsum(
        "htl,lhd->thd", weights, value_rows.astype(jnp.float32), precision=lax.Precision.HIGHEST
    )
    return (row_top, weight_sum, weighted)


def join_parts(earlier, later):
    joined = jnp.maximum(earlier[0], later[0])
    factor_one = jnp.exp(earlier[0] - joined)
    factor_two = jnp.exp(later[0] - joined)
    weight_sum = earlier[1] * factor_one + later[1] * factor_two
    weighted = (
        earlier[2] * jnp.transpose(factor_one)[:, :, None]
        + later[2] * jnp.transpose(factor_two)[:, :, None]
    )
    return (joined, weight_sum, weighted)


def page_attention(gathered, columns, queries, query_pos, length, slopes, heads_dev):
    number = gathered.shape[1]
    page_rows = gathered.shape[2]
    flat_pages = gathered.reshape(2, number * page_rows, heads_dev, HD)
    key_pos = (
        (columns[:, None] * page_rows + jnp.arange(page_rows)[None, :])
        .reshape(-1)
        .astype(jnp.float32)
    )
    allowed = jnp.broadcast_to(key_pos[None, :] < length, (queries.shape[0], key_pos.shape[0]))
    return partial_attention(
        queries, flat_pages[0], flat_pages[1], allowed, query_pos, key_pos, slopes
    )


def merge_softmax(earlier, later):
    joined = jnp.maximum(earlier[0], later[0])
    return (
        joined,
        earlier[1] * jnp.exp(earlier[0] - joined) + later[1] * jnp.exp(later[0] - joined),
        earlier[2] + later[2],
    )


def shards(
    residual,
    tree_qkv,
    kv_pool,
    page_table,
    cache_len,
    tree_parent,
    accepted_nodes,
    out_weight,
    norm_gain,
    draft_weight,
    vocab_weight,
    target_ids,
):
    lane_count = lax.axis_size("tp")
    lane_index = lax.axis_index("tp")
    group_index = lax.axis_index("group")
    partner = jnp.bitwise_xor(group_index, 1)
    heads_dev = HEADS // lane_count
    width_dev = residual.shape[1]
    slopes = slope_values(lane_index * heads_dev, heads_dev)
    odd_columns = jnp.arange(1, LONG_PAGES, 2, dtype=jnp.int32)
    attn_rows = []
    for slot_index in range(2):
        request = group_index * 2 + slot_index
        tree_block = tree_qkv[:, slot_index * TREE : (slot_index + 1) * TREE].reshape(
            3, TREE, heads_dev, HD
        )
        reached, depths = ancestry(tree_parent[request])
        length = cache_len[request].astype(jnp.float32)
        query_pos = length + depths
        merged = partial_attention(
            tree_block[0], tree_block[1], tree_block[2], reached > 0.5, query_pos, query_pos, slopes
        )
        table_row = page_table[request]
        if slot_index == 0:
            own_columns = jnp.arange(SHORT_PAGES, dtype=jnp.int32)
            own_slots = table_row[:SHORT_PAGES]
        else:
            own_columns = jnp.arange(0, LONG_PAGES, 2, dtype=jnp.int32)
            own_slots = table_row[0::2]
        own_pages = jnp.take(kv_pool, own_slots, axis=1)
        merged = join_parts(
            merged,
            page_attention(
                own_pages, own_columns, tree_block[0], query_pos, length, slopes, heads_dev
            ),
        )
        if slot_index == 1:
            guest_req = partner * 2 + 1
            visitors = from_partner(tree_block[0], "group", 0)
            guest_len = cache_len[guest_req].astype(jnp.float32)
            guest_pos = guest_len + ancestry(tree_parent[guest_req])[1]
            held_pages = jnp.take(kv_pool, page_table[guest_req][1::2], axis=1)
            guest_part = page_attention(
                held_pages, odd_columns, visitors, guest_pos, guest_len, slopes, heads_dev
            )
            returned = from_partner((guest_part[0], guest_part[1], guest_part[2]), "group", 0)
            merged = join_parts(merged, returned)
        row_top, weight_sum, weighted = merged
        attn_rows.append(
            (weighted / jnp.transpose(weight_sum)[:, :, None])
            .reshape(TREE, width_dev)
            .astype(jnp.bfloat16)
        )
    attn = jnp.concatenate(attn_rows, 0)
    head_term = jnp.dot(attn, out_weight, preferred_element_type=jnp.float32)
    head_share = lax.psum_scatter(
        head_term.astype(jnp.bfloat16), "tp", scatter_dimension=1, tiled=True
    ).astype(jnp.float32)
    hidden = residual.astype(jnp.float32) + head_share
    row_sums, squares = lax.psum((jnp.sum(hidden, axis=1), jnp.sum(hidden * hidden, axis=1)), "tp")
    row_mean = (row_sums / D)[:, None]
    row_var = (squares / D)[:, None] - row_mean * row_mean
    normed = ((hidden - row_mean) * lax.rsqrt(row_var + EPSILON) * norm_gain).astype(jnp.bfloat16)
    normed_full = lax.all_gather(normed, "tp", axis=1, tiled=True)
    updates = jnp.einsum(
        "td,kdc->ktc", normed_full, draft_weight, preferred_element_type=jnp.float32
    )
    drafted = (normed.astype(jnp.float32)[None] + jax.nn.silu(updates)).astype(jnp.bfloat16)
    vocab_dev = vocab_weight.shape[0]
    base_logits = lax.dot_general(
        vocab_weight, normed_full, (((1,), (1,)), ((), ())), preferred_element_type=jnp.float32
    )
    draft_logits = jnp.einsum(
        "vc,ktc->vkt",
        vocab_weight,
        lax.all_gather(drafted, "tp", axis=2, tiled=True),
        preferred_element_type=jnp.float32,
    )
    logits = jnp.concatenate([base_logits[:, None, :], draft_logits], 1)
    local_top = jnp.max(logits, axis=0)
    local_total = jnp.sum(jnp.exp(logits - local_top[None]), axis=0)
    vocab_ids = lane_index * vocab_dev + jnp.arange(vocab_dev, dtype=jnp.int32)
    matches = vocab_ids[:, None, None] == target_ids[None]
    local_pick = jnp.sum(jnp.where(matches, logits, 0.0), axis=0)
    global_top, global_total, picked = combined_all(
        (local_top, local_total, local_pick), "tp", merge_softmax
    )
    log_probs = picked - (global_top + jnp.log(global_total))
    flat_index = (jnp.arange(2, dtype=jnp.int32)[:, None] * TREE + accepted_nodes).reshape(-1)
    accepted_kv = jnp.take(tree_qkv[1:3], flat_index, axis=1)
    return (log_probs, accepted_kv)


def solution(mesh):
    placed = (
        P("group", "tp"),
        P(None, "group", "tp"),
        P(None, "group", None, "tp"),
        P(),
        P(),
        P(),
        P("group", None),
        P("tp", None),
        P("tp"),
        P(None, None, "tp"),
        P("tp", None),
        P(None, "group"),
    )
    return jax.shard_map(
        shards,
        mesh=mesh,
        in_specs=placed,
        out_specs=(P(None, "group"), P(None, "group", "tp")),
        check_vma=False,
    )
```

profile of v0, /device:TPU:0, one launch (start us, length us, event | category | flops | bytes accessed | tf_op | source)
XLA Modules:
  0.0 353.4 jit_solution(13451830431486187444)
XLA Ops:
  7.2 1.0 fusion.128
  11.9 1.4 fusion.129
  15.4 2.8 gather_fusion
  23.0 4.1 %gather_fusion.3 = bf16[14,2,128,256]{3,2,1,0:T(8,128)(2,1)} fusion(bf16[2,32,128,256]{3,2,1,0:T(8,128)(2,1)} %param.18, s32[1024]{0:T(1024)S(1)} %pad_clamp_fusion.1), kind=kCustom, calls=%fused_computation.1.clone | custom fusion | bytes 3670072 | tf_op jit(solution)/shard_map/jit(_take)/gather | solution.py:155
  27.2 1.7 select_bitcast_fusion
  28.9 1.1 fusion.126
  33.6 4.1 %gather_fusion.2 = bf16[14,2,128,256]{3,2,1,0:T(8,128)(2,1)} fusion(bf16[2,32,128,256]{3,2,1,0:T(8,128)(2,1)} %param.18, s32[1024]{0:T(1024)S(1)} %pad_clamp_fusion.2), kind=kCustom, calls=%fused_computation.clone | custom fusion | bytes 3670072 | tf_op jit(solution)/shard_map/jit(_take)/gather | solution.py:143
  37.7 1.7 select_bitcast_fusion.1
  39.4 1.4 fusion.125
  40.8 2.9 squeeze.97
  47.6 1.4 copy.48
  49.6 1.7 select_reduce_fusion.2
  52.1 1.5 fusion.31
  55.1 1.3 select_reduce_fusion.3
  57.2 0.9 select_reduce_fusion.5
  58.9 1.3 fusion.22
  61.9 1.0 fusion.24
  63.7 2.9 squeeze.100
  66.6 1.1 squeeze.101
  67.7 2.2 squeeze.98
  70.0 1.8 select_reduce_fusion.1
  75.6 1.4 convolution_convert_fusion
  77.2 75.3 %reduce-scatter.2.cloned.1.call-done = bf16[96,256]{1,0:T(8,128)(2,1)} async-done(((bf16[96,4096]{1,0:T(8,128)(2,1)}), bf16[96,256]{1,0:T(8,128)(2,1)}) %reduce-scatter.2.cloned.1.call-update) | async-done | bytes 49168 | tf_op jit(solution)/shard_map/reduce_scatter | solution.py:169
  153.4 38.1 %all-reduce = (f32[96]{0:T(128)S(1)}, f32[96]{0:T(128)S(1)}) all-reduce(f32[96]{0:T(128)S(1)} %get-tuple-element.191, f32[96]{0:T(128)S(1)} %get-tuple-element.190), channel_id=1, replica_groups=mesh['group'=8,'tp'=16] {'tp'}, use_global_device_ids=true, to_apply=%region_17.19 | all-reduce | flops 192 | bytes 1536 | tf_op jit(solution)/shard_map/psum | solution.py:173
  192.4 21.9 %all_gather.24 = bf16[96,4096]{1,0:T(8,128)(2,1)S(1)} all-gather(bf16[96,256]{1,0:T(8,128)(2,1)S(1)} %get-tuple-element.211), channel_id=1, replica_groups=mesh['group'=8,'tp'=16] {'tp'}, dimensions={1}, use_global_device_ids=true | all-gather | bytes 835584 | tf_op jit(solution)/shard_map/all_gather | solution.py:177
  214.4 4.7 %add_convert_fusion = bf16[3,96,256]{2,1,0:T(8,128)(2,1)} fusion(bf16[3,4096,256]{2,1,0:T(8,128)(2,1)} %param.25, bf16[96,4096]{1,0:T(8,128)(2,1)S(1)} %all_gather.24, f32[96,256]{1,0:T(8,128)S(1)} %get-tuple-element.210), kind=kOutput, calls=%fused_computation.86 | convolution fusion | flops 604422144 | bytes 7323648 | tf_op jit(solution)/shard_map/td,kdc->ktc/dot_general | solution.py:178
  220.7 9.1 %convolution_bitcast_fusion = f32[1664,1,96]{0,2,1:T(8,128)S(1)} fusion(bf16[96,4096]{1,0:T(8,128)(2,1)S(1)} %all_gather.24, bf16[1664,4096]{1,0:T(8,128)(2,1)} %param.26), kind=kOutput, calls=%fused_computation.23 | convolution fusion | flops 1308622848 | bytes 15056896 | tf_op jit(solution)/shard_map/dot_general | solution.py:183
  229.8 38.5 %all-gather.8.cloned.1.call-done = bf16[3,96,4096]{2,1,0:T(8,128)(2,1)} async-done(((bf16[3,96,256]{2,1,0:T(8,128)(2,1)}), bf16[3,96,4096]{2,1,0:T(8,128)(2,1)}) %all-gather.8.cloned.1.call-update) | async-done | bytes 2359312 | tf_op jit(solution)/shard_map/all_gather | solution.py:189
  268.3 9.1 %fusion.4 = f32[1664,3,96]{0,2,1:T(8,128)S(1)} fusion(bf16[3,96,4096]{2,1,0:T(8,128)(2,1)} %all-gather.8.cloned.1.call-done, bf16[1664,4096]{1,0:T(8,128)(2,1)} %param.26), kind=kOutput, calls=%fused_computation.13 | convolution fusion | flops 3925868544 | bytes 17907712 | tf_op jit(solution)/shard_map/vc,ktc->vkt/dot_general | solution.py:186
  278.9 22.6 %all-gather.5 = f32[16,4,96]{2,1,0:T(4,128)S(1)} all-gather(f32[1,4,96]{2,1,0:T(4,128)S(1)} %bitcast.234), channel_id=4, replica_groups=mesh['group'=8,'tp'=16] {'tp'}, dimensions={0}, use_global_device_ids=true | all-gather | bytes 26112 | tf_op jit(solution)/shard_map/all_gather | solution.py:27
  301.6 21.1 %all-gather.4 = f32[16,4,96]{2,1,0:T(4,128)S(1)} all-gather(f32[1,4,96]{2,1,0:T(4,128)S(1)} %bitcast.233), channel_id=3, replica_groups=mesh['group'=8,'tp'=16] {'tp'}, dimensions={0}, use_global_device_ids=true | all-gather | bytes 26112 | tf_op jit(solution)/shard_map/all_gather | solution.py:27
  322.7 22.6 %all-gather.3 = f32[16,4,96]{2,1,0:T(4,128)S(1)} all-gather(f32[1,4,96]{2,1,0:T(4,128)S(1)} %bitcast.232), channel_id=2, replica_groups=mesh['group'=8,'tp'=16] {'tp'}, dimensions={0}, use_global_device_ids=true | all-gather | bytes 26112 | tf_op jit(solution)/shard_map/all_gather | solution.py:27
  (166 shorter events, 33.7 us)
Async XLA Ops:
  7.2 68.4 %copy-start = (bf16[256,4096]{1,0:T(8,128)(2,1)S(1)}, bf16[256,4096]{1,0:T(8,128)(2,1)}, u32[]{:S(2)}) copy-start(bf16[256,4096]{1,0:T(8,128)(2,1)} %param.23) | copy-start | bytes 6291460
  7.2 145.3 %reduce-scatter.2.cloned.1.call-start = ((), (), s32[]{:S(2)}) async-start(), calls=%async_computation.1 | async-start | bytes 835584 | tf_op jit(solution)/shard_map/reduce_scatter | solution.py:169
  8.8 61.1 %collective-permute-start = (bf16[48,2,128]{2,0,1:T(8,128)(2,1)}, bf16[48,2,128]{2,0,1:T(8,128)(2,1)}, u32[]{:S(2)}, u32[]{:S(2)}) collective-permute-start(bf16[48,2,128]{2,0,1:T(8,128)(2,1)} %copy.49), channel_id=1, source_target_pairs={{0,16},{16,0},{32,48},{48,32},{64,80},{80,64},{96,112},{112,96},{1... | collective-permute-start | bytes 73736 | tf_op jit(solution)/shard_map/ppermute | solution.py:23
  49.6 4.0 %copy-start.5 = (pred[48,48]{0,1:T(8,128)(4,1)S(1)}, pred[48,48]{0,1:T(8,128)(4,1)}, u32[]{:S(2)}) copy-start(pred[48,48]{0,1:T(8,128)(4,1)} %copy.48) | copy-start | bytes 6916
  49.6 4.0 %copy-start.6 = (f32[48,48]{0,1:T(8,128)S(1)}, f32[48,48]{0,1:T(8,128)}, u32[]{:S(2)}) copy-start(f32[48,48]{0,1:T(8,128)} %broadcast_subtract_fusion.3) | copy-start | bytes 27652
  49.6 4.0 %copy-start.7 = (bf16[48,2,128]{2,1,0:T(2,128)(2,1)S(1)}, bf16[48,2,128]{2,1,0:T(2,128)(2,1)}, u32[]{:S(2)}) copy-start(bf16[48,2,128]{2,1,0:T(2,128)(2,1)} %squeeze.94) | copy-start | bytes 73732
  51.3 0.9 copy-start.2
  51.3 3.8 %copy-start.10 = (f32[2,48]{1,0:T(2,128)}, f32[2,48]{1,0:T(2,128)S(1)}, u32[]{:S(2)}) copy-start(f32[2,48]{1,0:T(2,128)S(1)} %get-tuple-element.250) | copy-start | bytes 1156
  54.4 4.4 %copy-start.8 = (f32[2,48]{1,0:T(2,128)}, f32[2,48]{1,0:T(2,128)S(1)}, u32[]{:S(2)}) copy-start(f32[2,48]{1,0:T(2,128)S(1)} %get-tuple-element.248) | copy-start | bytes 1156
  63.6 6.3 %copy-start.12 = (pred[1792]{0:T(1024)(128)(4,1)S(1)}, pred[1792]{0:T(1024)(128)(4,1)}, u32[]{:S(2)}) copy-start(pred[1792]{0:T(1024)(128)(4,1)} %broadcast_compare_fusion.2) | copy-start | bytes 5380
  63.6 6.3 %copy-start.19 = (f32[2]{0:T(128)S(1)}, f32[2]{0:T(128)}, u32[]{:S(2)}) copy-start(f32[2]{0:T(128)} %multiply_exponential_fusion) | copy-start | bytes 28
  69.9 2.8 copy-start.1
  69.9 4.1 %copy-start.9 = (f32[2,48]{1,0:T(2,128)S(1)}, f32[2,48]{1,0:T(2,128)}, u32[]{:S(2)}) copy-start(f32[2,48]{1,0:T(2,128)} %copy-done.8) | copy-start | bytes 1156
  69.9 4.1 %copy-start.11 = (f32[2,48]{1,0:T(2,128)S(1)}, f32[2,48]{1,0:T(2,128)}, u32[]{:S(2)}) copy-start(f32[2,48]{1,0:T(2,128)} %copy-done.10) | copy-start | bytes 1156
  69.9 4.1 %copy-start.14 = (f32[2,48]{1,0:T(2,128)S(1)}, f32[2,48]{1,0:T(2,128)}, u32[]{:S(2)}) copy-start(f32[2,48]{1,0:T(2,128)} %fusion.31) | copy-start | bytes 1156
  69.9 4.9 %copy-start.3 = (f32[2,48,1792]{2,1,0:T(8,128)S(1)}, f32[2,48,1792]{2,1,0:T(8,128)}, u32[]{:S(2)}) copy-start(f32[2,48,1792]{2,1,0:T(8,128)} %copy-done.2) | copy-start | bytes 2064388
  69.9 4.9 %copy-start.13 = (pred[1792]{0:T(1024)(128)(4,1)S(1)}, pred[1792]{0:T(1024)(128)(4,1)}, u32[]{:S(2)}) copy-start(pred[1792]{0:T(1024)(128)(4,1)} %broadcast_compare_fusion.3) | copy-start | bytes 5380
  69.9 4.9 %copy-start.18 = (f32[48,2]{0,1:T(2,128)S(1)}, f32[48,2]{0,1:T(2,128)}, u32[]{:S(2)}) copy-start(f32[48,2]{0,1:T(2,128)} %get-tuple-element.237) | copy-start | bytes 1156
  71.8 2.2 collective-permute-start.1
  72.6 1.3 collective-permute-start.3
  73.4 1.4 collective-permute-start.2
  75.6 76.9 %copy-start.4 = (bf16[96,256]{1,0:T(8,128)(2,1)S(1)}, bf16[96,256]{1,0:T(8,128)(2,1)}, u32[]{:S(2)}) copy-start(bf16[96,256]{1,0:T(8,128)(2,1)} %param.16) | copy-start | bytes 147460
  75.6 116.0 %copy-start.16 = (f32[256]{0:T(256)S(1)}, f32[256]{0:T(256)}, u32[]{:S(2)}) copy-start(f32[256]{0:T(256)} %param.24) | copy-start | bytes 3076
  77.0 191.3 %all-gather.8.cloned.1.call-start = ((), (), s32[]{:S(2)}) async-start(), calls=%async_computation.2 | async-start | bytes 2506752 | tf_op jit(solution)/shard_map/all_gather | solution.py:189
  214.4 4.7 %copy-start.17 = (s32[2,4]{1,0:T(2,128)S(1)}, s32[2,4]{1,0:T(2,128)}, u32[]{:S(2)}) copy-start(s32[2,4]{1,0:T(2,128)} %param.22) | copy-start | bytes 100
  214.4 5.0 %slice-start = ((bf16[3,96,256]{2,1,0:T(8,128)(2,1)}), bf16[2,96,256]{2,1,0:T(8,128)(2,1)S(1)}, s32[]{:S(2)}) async-start(bf16[3,96,256]{2,1,0:T(8,128)(2,1)} %param.17), calls=%async_computation.3 | async-start | bytes 196608 | tf_op jit(solution)/shard_map/slice | solution.py:203
  277.4 0.7 copy-start.15
Sparse Core Ops, SparseCore 0:
  77.1 75.3 reduce-scatter.1
  219.2 49.0 all-gather.7
where the time goes:
time: 355 us; the launch traced here: 353 us
  blocking collectives  126 us (35%)
  waiting for transfers between devices  115 us (32%)
  matrix products  38.7 us (11%)
  local copies, waits for them, and re-layouts  36.3 us (10%)
  other arithmetic  19.1 us (5%)
  between operations  16.6 us (5%)
    reduce_scatter x1, waiting for transfers between devices, shards(): lax.psum_scatter(head_term.astype(jnp.bfloat16), 'tp', scatter_dimension=...  75.3 us
    all_gather x3, blocking collectives, combined_all(): everything = jax.tree.map(lambda part: lax.all_gather(part, axis), array)  66.4 us
    all_gather x1, waiting for transfers between devices, shards(): lax.all_gather(drafted, 'tp', axis=2, tiled=True)  38.5 us
    psum x1, blocking collectives, shards(): lax.psum((jnp.sum(hidden, axis=1), jnp.sum(hidden * hidden, axis=1)), 'tp')  38.1 us
    all_gather x1, blocking collectives, shards(): normed_full = lax.all_gather(normed, 'tp', axis=1, tiled=True)  21.9 us
    dot_general x1, matrix products, shards(): jnp.einsum('vc,ktc->vkt', vocab_weight, lax.all_gather(drafted, 'tp', axi...  9.1 us
    dot_general x1, matrix products, shards(): lax.dot_general(vocab_weight, normed_full, (((1,), (1,)), ((), ())), pref...  9.1 us
  transfers between devices with their start and end apart: 6, of which 3 were waited for; matrix products, arithmetic and copies ran while one was open for 20% of the time, Pallas kernels for 0%

commit v1 on v0

--- a/solution.py
+++ b/solution.py
@@ -11,6 +11,24 @@
 SHORT_PAGES = 4
 LONG_PAGES = 28
 EPSILON = 1e-05
+
+
+def gather_around(value, axis, dim):
+    ways, here, step = (lax.axis_size(axis), lax.axis_index(axis), value.shape[dim])
+    shape = [n * ways if d == dim else n for d, n in enumerate(value.shape)]
+    full = lax.dynamic_update_slice_in_dim(
+        jnp.zeros(shape, value.dtype), value, here * step, axis=dim
+    )
+    going_up = going_down = value
+    for far in range(1, ways // 2 + 1):
+        going_up = lax.ppermute(going_up, axis, [(d, (d + 1) % ways) for d in range(ways)])
+        full = lax.dynamic_update_slice_in_dim(full, going_up, (here - far) % ways * step, axis=dim)
+        if 2 * far < ways:
+            going_down = lax.ppermute(going_down, axis, [(d, (d - 1) % ways) for d in range(ways)])
+            full = lax.dynamic_update_slice_in_dim(
+                full, going_down, (here + far) % ways * step, axis=dim
+            )
+    return full
 
 
 def from_partner(block, axis, apart):
@@ -174,7 +192,7 @@
     row_mean = (row_sums / D)[:, None]
     row_var = (squares / D)[:, None] - row_mean * row_mean
     normed = ((hidden - row_mean) * lax.rsqrt(row_var + EPSILON) * norm_gain).astype(jnp.bfloat16)
-    normed_full = lax.all_gather(normed, "tp", axis=1, tiled=True)
+    normed_full = gather_around(normed, "tp", 1)
     updates = jnp.einsum(
         "td,kdc->ktc", normed_full, draft_weight, preferred_element_type=jnp.float32
     )

time: 355 us -> 389 us (1.096)
  starting transfers between devices: 1.46 us -> 40 us
  blocking collectives: 126 us -> 104 us
  waiting for transfers between devices: 115 us -> 131 us
    ppermute x0 -> x15, starting transfers between devices: none -> 38.5 us  [the longest x7 38.4 us: gather_around(): lax.ppermute(going_down, axis, [(d, (d - 1) % ways) for d in range(ways)])]
    all_gather x1 -> x0, blocking collectives: 21.9 us -> none  [shards(): normed_full = lax.all_gather(normed, 'tp', axis=1, tiled=True)]
    ppermute x0 -> x15, waiting for transfers between devices: none -> 20.8 us  [the longest x8 20.8 us: gather_around(): lax.ppermute(going_up, axis, [(d, (d + 1) % ways) for d in range(ways)])]
    all_gather x1, waiting for transfers between devices: 38.5 us -> 34.5 us  [shards(): lax.all_gather(drafted, 'tp', axis=2, tiled=True)]
  transfers between devices with their start and end apart: 6 -> 21, of which waited for: 3 -> 11; matrix products, arithmetic and copies ran while one was open for 20% -> 18% of each run, Pallas kernels for 0% -> 0%
where the time goes in v1:
time: 389 us; the launch traced here: 387 us
  waiting for transfers between devices  131 us (34%)
  blocking collectives  104 us (27%)
  starting transfers between devices  40 us (10%)
  matrix products  38.7 us (10%)
  local copies, waits for them, and re-layouts  36.6 us (9%)
  other arithmetic  19.2 us (5%)
  between operations  17 us (4%)
    reduce_scatter x1, waiting for transfers between devices, shards(): lax.psum_scatter(head_term.astype(jnp.bfloat16), 'tp', scatter_dimension=...  74.9 us
    all_gather x3, blocking collectives, combined_all(): everything = jax.tree.map(lambda part: lax.all_gather(part, axis), array)  66.4 us
    ppermute x7, starting transfers between devices, gather_around(): lax.ppermute(going_down, axis, [(d, (d - 1) % ways) for d in range(ways)])  38.4 us
    psum x1, blocking collectives, shards(): lax.psum((jnp.sum(hidden, axis=1), jnp.sum(hidden * hidden, axis=1)), 'tp')  38.1 us
    all_gather x1, waiting for transfers between devices, shards(): lax.all_gather(drafted, 'tp', axis=2, tiled=True)  34.5 us
    ppermute x8, waiting for transfers between devices, gather_around(): lax.ppermute(going_up, axis, [(d, (d + 1) % ways) for d in range(ways)])  20.8 us
    dot_general x1, matrix products, shards(): lax.dot_general(vocab_weight, normed_full, (((1,), (1,)), ((), ())), pref...  9.17 us
    dot_general x1, matrix products, shards(): jnp.einsum('vc,ktc->vkt', vocab_weight, lax.all_gather(drafted, 'tp', axi...  9.1 us
  transfers between devices with their start and end apart: 21, of which 11 were waited for; matrix products, arithmetic and copies ran while one was open for 18% of the time, Pallas kernels for 0%

profile of v1, /device:TPU:0, one launch (start us, length us, event | category | flops | bytes accessed | tf_op | source)
XLA Modules:
  0.0 387.4 jit_solution(4651042847714952508)
XLA Ops:
  15.5 2.8 gather_fusion
  23.1 4.1 %gather_fusion.3 = bf16[14,2,128,256]{3,2,1,0:T(8,128)(2,1)} fusion(bf16[2,32,128,256]{3,2,1,0:T(8,128)(2,1)} %param.18, s32[1024]{0:T(1024)S(1)} %pad_clamp_fusion.1), kind=kCustom, calls=%fused_computation.1.clone | custom fusion | bytes 3670072 | tf_op jit(solution)/shard_map/jit(_take)/gather | solution.py:173
  27.2 1.7 select_bitcast_fusion
  33.7 4.1 %gather_fusion.2 = bf16[14,2,128,256]{3,2,1,0:T(8,128)(2,1)} fusion(bf16[2,32,128,256]{3,2,1,0:T(8,128)(2,1)} %param.18, s32[1024]{0:T(1024)S(1)} %pad_clamp_fusion.2), kind=kCustom, calls=%fused_computation.clone | custom fusion | bytes 3670072 | tf_op jit(solution)/shard_map/jit(_take)/gather | solution.py:161
  40.9 2.9 squeeze.97
  63.9 2.9 squeeze.100
  67.9 2.2 squeeze.98
  70.2 1.8 select_reduce_fusion.1
  77.7 74.9 %reduce-scatter.2.cloned.1.call-done = bf16[96,256]{1,0:T(8,128)(2,1)} async-done(((bf16[96,4096]{1,0:T(8,128)(2,1)}), bf16[96,256]{1,0:T(8,128)(2,1)}) %reduce-scatter.2.cloned.1.call-update) | async-done | bytes 49168 | tf_op jit(solution)/shard_map/reduce_scatter | solution.py:187
  153.6 38.1 %all-reduce = (f32[96]{0:T(128)S(1)}, f32[96]{0:T(128)S(1)}) all-reduce(f32[96]{0:T(128)S(1)} %get-tuple-element.191, f32[96]{0:T(128)S(1)} %get-tuple-element.190), channel_id=1, replica_groups=mesh['group'=8,'tp'=16] {'tp'}, use_global_device_ids=true, to_apply=%region_17.19 | all-reduce | flops 192 | bytes 1536 | tf_op jit(solution)/shard_map/psum | solution.py:191
  192.7 5.3 %collective-permute-start.5 = (bf16[96,256]{1,0:T(8,128)(2,1)S(1)}, bf16[96,256]{1,0:T(8,128)(2,1)S(1)}, u32[]{:S(2)}, u32[]{:S(2)}) collective-permute-start(bf16[96,256]{1,0:T(8,128)(2,1)S(1)} %get-tuple-element.211), channel_id=1, source_target_pairs={{0,15},{1,0},{2,1},{3,2},{4,3},{5,4},{6,5},{7,6},{8,7},{9,8},{10,9... | collective-permute-start | bytes 147464 | tf_op jit(solution)/shard_map/ppermute | solution.py:27
  198.1 2.0 collective-permute-done.4
  200.1 5.3 %collective-permute-start.7 = (bf16[96,256]{1,0:T(8,128)(2,1)S(1)}, bf16[96,256]{1,0:T(8,128)(2,1)S(1)}, u32[]{:S(2)}, u32[]{:S(2)}) collective-permute-start(bf16[96,256]{1,0:T(8,128)(2,1)S(1)} %collective-permute-done.5), channel_id=1, source_target_pairs={{0,15},{1,0},{2,1},{3,2},{4,3},{5,4},{6,5},{7,6},{8,7},{9,8},{10,9... | collective-permute-start | bytes 147464 | tf_op jit(solution)/shard_map/ppermute | solution.py:27
  205.4 2.0 collective-permute-done.6
  207.5 5.3 %collective-permute-start.9 = (bf16[96,256]{1,0:T(8,128)(2,1)S(1)}, bf16[96,256]{1,0:T(8,128)(2,1)S(1)}, u32[]{:S(2)}, u32[]{:S(2)}) collective-permute-start(bf16[96,256]{1,0:T(8,128)(2,1)S(1)} %collective-permute-done.7), channel_id=1, source_target_pairs={{0,15},{1,0},{2,1},{3,2},{4,3},{5,4},{6,5},{7,6},{8,7},{9,8},{10,9... | collective-permute-start | bytes 147464 | tf_op jit(solution)/shard_map/ppermute | solution.py:27
  212.8 2.3 collective-permute-done.8
  215.2 5.6 %collective-permute-start.11 = (bf16[96,256]{1,0:T(8,128)(2,1)S(1)}, bf16[96,256]{1,0:T(8,128)(2,1)S(1)}, u32[]{:S(2)}, u32[]{:S(2)}) collective-permute-start(bf16[96,256]{1,0:T(8,128)(2,1)S(1)} %collective-permute-done.9), channel_id=1, source_target_pairs={{0,15},{1,0},{2,1},{3,2},{4,3},{5,4},{6,5},{7,6},{8,7},{9,8},{10,9... | collective-permute-start | bytes 147464 | tf_op jit(solution)/shard_map/ppermute | solution.py:27
  220.8 1.8 collective-permute-done.10
  222.6 5.6 %collective-permute-start.13 = (bf16[96,256]{1,0:T(8,128)(2,1)S(1)}, bf16[96,256]{1,0:T(8,128)(2,1)S(1)}, u32[]{:S(2)}, u32[]{:S(2)}) collective-permute-start(bf16[96,256]{1,0:T(8,128)(2,1)S(1)} %collective-permute-done.11), channel_id=1, source_target_pairs={{0,15},{1,0},{2,1},{3,2},{4,3},{5,4},{6,5},{7,6},{8,7},{9,8},{10,9... | collective-permute-start | bytes 147464 | tf_op jit(solution)/shard_map/ppermute | solution.py:27
  228.2 1.8 collective-permute-done.12
  230.0 5.6 %collective-permute-start.15 = (bf16[96,256]{1,0:T(8,128)(2,1)S(1)}, bf16[96,256]{1,0:T(8,128)(2,1)S(1)}, u32[]{:S(2)}, u32[]{:S(2)}) collective-permute-start(bf16[96,256]{1,0:T(8,128)(2,1)S(1)} %collective-permute-done.13), channel_id=1, source_target_pairs={{0,15},{1,0},{2,1},{3,2},{4,3},{5,4},{6,5},{7,6},{8,7},{9,8},{10,9... | collective-permute-start | bytes 147464 | tf_op jit(solution)/shard_map/ppermute | solution.py:27
  235.6 1.8 collective-permute-done.14
  237.4 5.6 %collective-permute-start.17 = (bf16[96,256]{1,0:T(8,128)(2,1)S(1)}, bf16[96,256]{1,0:T(8,128)(2,1)S(1)}, u32[]{:S(2)}, u32[]{:S(2)}) collective-permute-start(bf16[96,256]{1,0:T(8,128)(2,1)S(1)} %collective-permute-done.15), channel_id=1, source_target_pairs={{0,15},{1,0},{2,1},{3,2},{4,3},{5,4},{6,5},{7,6},{8,7},{9,8},{10,9... | collective-permute-start | bytes 147464 | tf_op jit(solution)/shard_map/ppermute | solution.py:27
  243.0 1.8 collective-permute-done.16
  244.8 7.4 %collective-permute-done.18 = bf16[96,256]{1,0:T(8,128)(2,1)S(1)} collective-permute-done((bf16[96,256]{1,0:T(8,128)(2,1)S(1)}, bf16[96,256]{1,0:T(8,128)(2,1)S(1)}, u32[]{:S(2)}, u32[]{:S(2)}) %collective-permute-start.18) | collective-permute-done | bytes 49184 | tf_op jit(solution)/shard_map/ppermute | solution.py:24
  252.2 4.7 %add_convert_fusion = bf16[3,96,256]{2,1,0:T(8,128)(2,1)} fusion(bf16[3,4096,256]{2,1,0:T(8,128)(2,1)} %param.25, bf16[96,4096]{1,0:T(8,128)(2,1)S(1)} %constant_dynamic-update-slice_fusion, f32[96,256]{1,0:T(8,128)S(1)} %get-tuple-element.210), kind=kOutput, calls=%fused_computation.86 | convolution fusion | flops 604422144 | bytes 7323648 | tf_op jit(solution)/shard_map/td,kdc->ktc/dot_general | solution.py:196
  258.6 9.2 %convolution_bitcast_fusion = f32[1664,1,96]{0,2,1:T(8,128)S(1)} fusion(bf16[96,4096]{1,0:T(8,128)(2,1)S(1)} %constant_dynamic-update-slice_fusion, bf16[1664,4096]{1,0:T(8,128)(2,1)} %param.26), kind=kOutput, calls=%fused_computation.23 | convolution fusion | flops 1308622848 | bytes 15056896 | tf_op jit(solution)/shard_map/dot_general | solution.py:201
  267.8 34.5 %all-gather.8.cloned.1.call-done = bf16[3,96,4096]{2,1,0:T(8,128)(2,1)} async-done(((bf16[3,96,256]{2,1,0:T(8,128)(2,1)}), bf16[3,96,4096]{2,1,0:T(8,128)(2,1)}) %all-gather.8.cloned.1.call-update) | async-done | bytes 2359312 | tf_op jit(solution)/shard_map/all_gather | solution.py:207
  302.3 9.1 %fusion.4 = f32[1664,3,96]{0,2,1:T(8,128)S(1)} fusion(bf16[3,96,4096]{2,1,0:T(8,128)(2,1)} %all-gather.8.cloned.1.call-done, bf16[1664,4096]{1,0:T(8,128)(2,1)} %param.26), kind=kOutput, calls=%fused_computation.13 | convolution fusion | flops 3925868544 | bytes 17907712 | tf_op jit(solution)/shard_map/vc,ktc->vkt/dot_general | solution.py:204
  312.9 22.6 %all-gather.5 = f32[16,4,96]{2,1,0:T(4,128)S(1)} all-gather(f32[1,4,96]{2,1,0:T(4,128)S(1)} %bitcast.234), channel_id=4, replica_groups=mesh['group'=8,'tp'=16] {'tp'}, dimensions={0}, use_global_device_ids=true | all-gather | bytes 26112 | tf_op jit(solution)/shard_map/all_gather | solution.py:45
  335.5 21.1 %all-gather.4 = f32[16,4,96]{2,1,0:T(4,128)S(1)} all-gather(f32[1,4,96]{2,1,0:T(4,128)S(1)} %bitcast.233), channel_id=3, replica_groups=mesh['group'=8,'tp'=16] {'tp'}, dimensions={0}, use_global_device_ids=true | all-gather | bytes 26112 | tf_op jit(solution)/shard_map/all_gather | solution.py:45
  356.7 22.6 %all-gather.3 = f32[16,4,96]{2,1,0:T(4,128)S(1)} all-gather(f32[1,4,96]{2,1,0:T(4,128)S(1)} %bitcast.232), channel_id=2, replica_groups=mesh['group'=8,'tp'=16] {'tp'}, dimensions={0}, use_global_device_ids=true | all-gather | bytes 26112 | tf_op jit(solution)/shard_map/all_gather | solution.py:45
  (212 shorter events, 52.1 us)
Async XLA Ops:
  7.2 68.6 %copy-start = (bf16[256,4096]{1,0:T(8,128)(2,1)S(1)}, bf16[256,4096]{1,0:T(8,128)(2,1)}, u32[]{:S(2)}) copy-start(bf16[256,4096]{1,0:T(8,128)(2,1)} %param.23) | copy-start | bytes 6291460
  7.2 145.5 %reduce-scatter.2.cloned.1.call-start = ((), (), s32[]{:S(2)}) async-start(), calls=%async_computation.1 | async-start | bytes 835584 | tf_op jit(solution)/shard_map/reduce_scatter | solution.py:187
  8.8 61.3 %collective-permute-start = (bf16[48,2,128]{2,0,1:T(8,128)(2,1)}, bf16[48,2,128]{2,0,1:T(8,128)(2,1)}, u32[]{:S(2)}, u32[]{:S(2)}) collective-permute-start(bf16[48,2,128]{2,0,1:T(8,128)(2,1)} %copy.49), channel_id=1, source_target_pairs={{0,16},{16,0},{32,48},{48,32},{64,80},{80,64},{96,112},{112,96},{1... | collective-permute-start | bytes 73736 | tf_op jit(solution)/shard_map/ppermute | solution.py:41
  54.7 4.4 %copy-start.8 = (f32[2,48]{1,0:T(2,128)}, f32[2,48]{1,0:T(2,128)S(1)}, u32[]{:S(2)}) copy-start(f32[2,48]{1,0:T(2,128)S(1)} %get-tuple-element.248) | copy-start | bytes 1156
  63.8 6.3 %copy-start.12 = (pred[1792]{0:T(1024)(128)(4,1)S(1)}, pred[1792]{0:T(1024)(128)(4,1)}, u32[]{:S(2)}) copy-start(pred[1792]{0:T(1024)(128)(4,1)} %broadcast_compare_fusion.2) | copy-start | bytes 5380
  63.9 6.3 %copy-start.19 = (f32[2]{0:T(128)S(1)}, f32[2]{0:T(128)}, u32[]{:S(2)}) copy-start(f32[2]{0:T(128)} %multiply_exponential_fusion) | copy-start | bytes 28
  70.1 4.9 %copy-start.3 = (f32[2,48,1792]{2,1,0:T(8,128)S(1)}, f32[2,48,1792]{2,1,0:T(8,128)}, u32[]{:S(2)}) copy-start(f32[2,48,1792]{2,1,0:T(8,128)} %copy-done.2) | copy-start | bytes 2064388
  70.1 4.9 %copy-start.13 = (pred[1792]{0:T(1024)(128)(4,1)S(1)}, pred[1792]{0:T(1024)(128)(4,1)}, u32[]{:S(2)}) copy-start(pred[1792]{0:T(1024)(128)(4,1)} %broadcast_compare_fusion.3) | copy-start | bytes 5380
  70.2 4.9 %copy-start.18 = (f32[48,2]{0,1:T(2,128)S(1)}, f32[48,2]{0,1:T(2,128)}, u32[]{:S(2)}) copy-start(f32[48,2]{0,1:T(2,128)} %get-tuple-element.237) | copy-start | bytes 1156
  72.0 2.2 collective-permute-start.1
  72.8 1.3 collective-permute-start.3
  73.6 1.4 collective-permute-start.2
  75.8 76.9 %copy-start.4 = (bf16[96,256]{1,0:T(8,128)(2,1)S(1)}, bf16[96,256]{1,0:T(8,128)(2,1)}, u32[]{:S(2)}) copy-start(bf16[96,256]{1,0:T(8,128)(2,1)} %param.16) | copy-start | bytes 147460
  75.8 115.9 %copy-start.16 = (f32[256]{0:T(256)S(1)}, f32[256]{0:T(256)}, u32[]{:S(2)}) copy-start(f32[256]{0:T(256)} %param.24) | copy-start | bytes 3076
  77.2 225.1 %all-gather.8.cloned.1.call-start = ((), (), s32[]{:S(2)}) async-start(), calls=%async_computation.2 | async-start | bytes 2506752 | tf_op jit(solution)/shard_map/all_gather | solution.py:207
  192.6 7.5 %collective-permute-start.4 = (bf16[96,256]{1,0:T(8,128)(2,1)S(1)}, bf16[96,256]{1,0:T(8,128)(2,1)S(1)}, u32[]{:S(2)}, u32[]{:S(2)}) collective-permute-start(bf16[96,256]{1,0:T(8,128)(2,1)S(1)} %get-tuple-element.211), channel_id=1, source_target_pairs={{0,1},{1,2},{2,3},{3,4},{4,5},{5,6},{6,7},{7,8},{8,9},{9,10},{10,1... | collective-permute-start | bytes 147464 | tf_op jit(solution)/shard_map/ppermute | solution.py:24
  192.7 7.4 %collective-permute-start.5 = (bf16[96,256]{1,0:T(8,128)(2,1)S(1)}, bf16[96,256]{1,0:T(8,128)(2,1)S(1)}, u32[]{:S(2)}, u32[]{:S(2)}) collective-permute-start(bf16[96,256]{1,0:T(8,128)(2,1)S(1)} %get-tuple-element.211), channel_id=1, source_target_pairs={{0,15},{1,0},{2,1},{3,2},{4,3},{5,4},{6,5},{7,6},{8,7},{9,8},{10,9... | collective-permute-start | bytes 147464 | tf_op jit(solution)/shard_map/ppermute | solution.py:27
  200.1 7.4 %collective-permute-start.6 = (bf16[96,256]{1,0:T(8,128)(2,1)S(1)}, bf16[96,256]{1,0:T(8,128)(2,1)S(1)}, u32[]{:S(2)}, u32[]{:S(2)}) collective-permute-start(bf16[96,256]{1,0:T(8,128)(2,1)S(1)} %collective-permute-done.4), channel_id=1, source_target_pairs={{0,1},{1,2},{2,3},{3,4},{4,5},{5,6},{6,7},{7,8},{8,9},{9,10},{10,1... | collective-permute-start | bytes 147464 | tf_op jit(solution)/shard_map/ppermute | solution.py:24
  200.1 7.4 %collective-permute-start.7 = (bf16[96,256]{1,0:T(8,128)(2,1)S(1)}, bf16[96,256]{1,0:T(8,128)(2,1)S(1)}, u32[]{:S(2)}, u32[]{:S(2)}) collective-permute-start(bf16[96,256]{1,0:T(8,128)(2,1)S(1)} %collective-permute-done.5), channel_id=1, source_target_pairs={{0,15},{1,0},{2,1},{3,2},{4,3},{5,4},{6,5},{7,6},{8,7},{9,8},{10,9... | collective-permute-start | bytes 147464 | tf_op jit(solution)/shard_map/ppermute | solution.py:27
  207.5 7.7 %collective-permute-start.8 = (bf16[96,256]{1,0:T(8,128)(2,1)S(1)}, bf16[96,256]{1,0:T(8,128)(2,1)S(1)}, u32[]{:S(2)}, u32[]{:S(2)}) collective-permute-start(bf16[96,256]{1,0:T(8,128)(2,1)S(1)} %collective-permute-done.6), channel_id=1, source_target_pairs={{0,1},{1,2},{2,3},{3,4},{4,5},{5,6},{6,7},{7,8},{8,9},{9,10},{10,1... | collective-permute-start | bytes 147464 | tf_op jit(solution)/shard_map/ppermute | solution.py:24
  207.5 7.7 %collective-permute-start.9 = (bf16[96,256]{1,0:T(8,128)(2,1)S(1)}, bf16[96,256]{1,0:T(8,128)(2,1)S(1)}, u32[]{:S(2)}, u32[]{:S(2)}) collective-permute-start(bf16[96,256]{1,0:T(8,128)(2,1)S(1)} %collective-permute-done.7), channel_id=1, source_target_pairs={{0,15},{1,0},{2,1},{3,2},{4,3},{5,4},{6,5},{7,6},{8,7},{9,8},{10,9... | collective-permute-start | bytes 147464 | tf_op jit(solution)/shard_map/ppermute | solution.py:27
  215.1 7.4 %collective-permute-start.10 = (bf16[96,256]{1,0:T(8,128)(2,1)S(1)}, bf16[96,256]{1,0:T(8,128)(2,1)S(1)}, u32[]{:S(2)}, u32[]{:S(2)}) collective-permute-start(bf16[96,256]{1,0:T(8,128)(2,1)S(1)} %collective-permute-done.8), channel_id=1, source_target_pairs={{0,1},{1,2},{2,3},{3,4},{4,5},{5,6},{6,7},{7,8},{8,9},{9,10},{10,1... | collective-permute-start | bytes 147464 | tf_op jit(solution)/shard_map/ppermute | solution.py:24
  215.2 7.4 %collective-permute-start.11 = (bf16[96,256]{1,0:T(8,128)(2,1)S(1)}, bf16[96,256]{1,0:T(8,128)(2,1)S(1)}, u32[]{:S(2)}, u32[]{:S(2)}) collective-permute-start(bf16[96,256]{1,0:T(8,128)(2,1)S(1)} %collective-permute-done.9), channel_id=1, source_target_pairs={{0,15},{1,0},{2,1},{3,2},{4,3},{5,4},{6,5},{7,6},{8,7},{9,8},{10,9... | collective-permute-start | bytes 147464 | tf_op jit(solution)/shard_map/ppermute | solution.py:27
  222.6 7.4 %collective-permute-start.12 = (bf16[96,256]{1,0:T(8,128)(2,1)S(1)}, bf16[96,256]{1,0:T(8,128)(2,1)S(1)}, u32[]{:S(2)}, u32[]{:S(2)}) collective-permute-start(bf16[96,256]{1,0:T(8,128)(2,1)S(1)} %collective-permute-done.10), channel_id=1, source_target_pairs={{0,1},{1,2},{2,3},{3,4},{4,5},{5,6},{6,7},{7,8},{8,9},{9,10},{10,1... | collective-permute-start | bytes 147464 | tf_op jit(solution)/shard_map/ppermute | solution.py:24
  222.6 7.4 %collective-permute-start.13 = (bf16[96,256]{1,0:T(8,128)(2,1)S(1)}, bf16[96,256]{1,0:T(8,128)(2,1)S(1)}, u32[]{:S(2)}, u32[]{:S(2)}) collective-permute-start(bf16[96,256]{1,0:T(8,128)(2,1)S(1)} %collective-permute-done.11), channel_id=1, source_target_pairs={{0,15},{1,0},{2,1},{3,2},{4,3},{5,4},{6,5},{7,6},{8,7},{9,8},{10,9... | collective-permute-start | bytes 147464 | tf_op jit(solution)/shard_map/ppermute | solution.py:27
  230.0 7.4 %collective-permute-start.14 = (bf16[96,256]{1,0:T(8,128)(2,1)S(1)}, bf16[96,256]{1,0:T(8,128)(2,1)S(1)}, u32[]{:S(2)}, u32[]{:S(2)}) collective-permute-start(bf16[96,256]{1,0:T(8,128)(2,1)S(1)} %collective-permute-done.12), channel_id=1, source_target_pairs={{0,1},{1,2},{2,3},{3,4},{4,5},{5,6},{6,7},{7,8},{8,9},{9,10},{10,1... | collective-permute-start | bytes 147464 | tf_op jit(solution)/shard_map/ppermute | solution.py:24
  230.0 7.4 %collective-permute-start.15 = (bf16[96,256]{1,0:T(8,128)(2,1)S(1)}, bf16[96,256]{1,0:T(8,128)(2,1)S(1)}, u32[]{:S(2)}, u32[]{:S(2)}) collective-permute-start(bf16[96,256]{1,0:T(8,128)(2,1)S(1)} %collective-permute-done.13), channel_id=1, source_target_pairs={{0,15},{1,0},{2,1},{3,2},{4,3},{5,4},{6,5},{7,6},{8,7},{9,8},{10,9... | collective-permute-start | bytes 147464 | tf_op jit(solution)/shard_map/ppermute | solution.py:27
  237.4 7.4 %collective-permute-start.16 = (bf16[96,256]{1,0:T(8,128)(2,1)S(1)}, bf16[96,256]{1,0:T(8,128)(2,1)S(1)}, u32[]{:S(2)}, u32[]{:S(2)}) collective-permute-start(bf16[96,256]{1,0:T(8,128)(2,1)S(1)} %collective-permute-done.14), channel_id=1, source_target_pairs={{0,1},{1,2},{2,3},{3,4},{4,5},{5,6},{6,7},{7,8},{8,9},{9,10},{10,1... | collective-permute-start | bytes 147464 | tf_op jit(solution)/shard_map/ppermute | solution.py:24
  237.4 7.4 %collective-permute-start.17 = (bf16[96,256]{1,0:T(8,128)(2,1)S(1)}, bf16[96,256]{1,0:T(8,128)(2,1)S(1)}, u32[]{:S(2)}, u32[]{:S(2)}) collective-permute-start(bf16[96,256]{1,0:T(8,128)(2,1)S(1)} %collective-permute-done.15), channel_id=1, source_target_pairs={{0,15},{1,0},{2,1},{3,2},{4,3},{5,4},{6,5},{7,6},{8,7},{9,8},{10,9... | collective-permute-start | bytes 147464 | tf_op jit(solution)/shard_map/ppermute | solution.py:27
  244.8 7.4 %collective-permute-start.18 = (bf16[96,256]{1,0:T(8,128)(2,1)S(1)}, bf16[96,256]{1,0:T(8,128)(2,1)S(1)}, u32[]{:S(2)}, u32[]{:S(2)}) collective-permute-start(bf16[96,256]{1,0:T(8,128)(2,1)S(1)} %collective-permute-done.16), channel_id=1, source_target_pairs={{0,1},{1,2},{2,3},{3,4},{4,5},{5,6},{6,7},{7,8},{8,9},{9,10},{10,1... | collective-permute-start | bytes 147464 | tf_op jit(solution)/shard_map/ppermute | solution.py:24
  252.2 4.7 %copy-start.17 = (s32[2,4]{1,0:T(2,128)S(1)}, s32[2,4]{1,0:T(2,128)}, u32[]{:S(2)}) copy-start(s32[2,4]{1,0:T(2,128)} %param.22) | copy-start | bytes 100
  252.2 5.0 %slice-start = ((bf16[3,96,256]{2,1,0:T(8,128)(2,1)}), bf16[2,96,256]{2,1,0:T(8,128)(2,1)S(1)}, s32[]{:S(2)}) async-start(bf16[3,96,256]{2,1,0:T(8,128)(2,1)} %param.17), calls=%async_computation.3 | async-start | bytes 196608 | tf_op jit(solution)/shard_map/slice | solution.py:221
  (10 other events, 32.5 us)
Sparse Core Ops, SparseCore 0:
  77.3 75.2 reduce-scatter.1
  257.0 45.2 all-gather.7
